TPU v7x, 32 devices: a whole 2x2x4 slice. The times are simulated.
32 devices in a mesh: section: 2 (over core), chan: 4 (over z), dp: 4 (over y, x).
Axes of the slice: x: 2, y: 2, z: 4, core: 2. Of those that a mesh axis runs over, the one named last changes fastest.
Arguments:
- inputs: bfloat16 [2, 16, 1024, 768], P(None, ('dp', 'chan')), may hold values from -6 to 6
- lengths: int32 [2, 16], P(None, ('dp', 'chan')), may hold values from 512 to 1024, as said below
- out_grad: bfloat16 [2, 16, 1024, 768], P(None, ('dp', 'chan')), may hold values from -6 to 6
- ln_mix_gain: bfloat16 [1, 768], P(None, 'chan'), may hold values from 0.5 to 1.5
- w_in: bfloat16 [1, 768, 2304], P(None, 'chan'), may hold values from -0.21875 to 0.21875
- short_taps: bfloat16 [1, 3, 2304], P(None, None, 'chan'), may hold values from -3 to 3
- long_taps: bfloat16 [1, 1024, 768], P(None, None, 'chan'), may hold values from -0.5 to 0.5
- w_out: bfloat16 [1, 768, 768], P(None, 'chan'), may hold values from -0.21875 to 0.21875
- ln_mlp_gain: bfloat16 [1, 768], P(None, 'chan'), may hold values from 0.5 to 1.5
- w_up: bfloat16 [1, 768, 3072], P(None, 'chan'), may hold values from -0.21875 to 0.21875
- w_down: bfloat16 [1, 3072, 768], P(None, 'chan'), may hold values from -0.109375 to 0.109375
Outputs:
- activations: bfloat16 [2, 2, 16, 1024, 768], P('section', None, ('dp', 'chan'))
- act_grads: float32 [2, 2, 16, 1024, 768], P('section', None, ('dp', 'chan'))
- grad_ln_mix_gain: float32 [1, 768], P(None, 'chan')
- grad_w_in: float32 [1, 768, 2304], P(None, 'chan')
- grad_short_taps: float32 [1, 3, 2304], P(None, None, 'chan')
- grad_long_taps: float32 [1, 1024, 768], P(None, None, 'chan')
- grad_w_out: float32 [1, 768, 768], P(None, 'chan')
- grad_ln_mlp_gain: float32 [1, 768], P(None, 'chan')
- grad_w_up: float32 [1, 768, 3072], P(None, 'chan')
- grad_w_down: float32 [1, 3072, 768], P(None, 'chan')
Inputs may be any that keep to these rules, and one draw needn't show every extreme that they name: `lengths`: in every micro-batch one slot holds 1024 live positions and another holds 512.
All inputs are finite; a program needn't handle non-finite values.
Results may differ from a plain program's by a relative error of at most 0.015.
Values may be sent and summed in bfloat16 or wider, within the bound.
No kernel may reach another device: no remote copies, remote signals or barrier semaphores. Data moves between devices by JAX's collectives and lax.ppermute only.
A program may use at most 384 MiB of HBM per device.

v0:
```python
import math

import jax
import jax.numpy as jnp
from jax import lax
from jax.sharding import PartitionSpec as P

D = 768
FF = 3072


decay_rate = 0.003
first_radix = 32
highest = lax.Precision.HIGHEST


def from_behind(value, axis, steps):
    count = lax.axis_size(axis)
    initial, last = (max(0, -steps), min(count, count - steps))
    return lax.ppermute(value, axis, [(source, source + steps) for source in range(initial, last)])


def layer_norm(values, gain_vec):
    centered = values - jnp.mean(values, axis=-1, keepdims=True)
    spread = jnp.mean(centered * centered, axis=-1, keepdims=True)
    return centered * lax.rsqrt(spread + 1e-05) * gain_vec


def twiddles(rows, columns, period, direction):
    row_ids = lax.broadcasted_iota(jnp.int32, (rows, columns), 0)
    col_ids = lax.broadcasted_iota(jnp.int32, (rows, columns), 1)
    phase = row_ids * col_ids % period
    angle = direction * 2.0 * math.pi * phase.astype(jnp.float32) / period
    return (jnp.cos(angle), jnp.sin(angle))


def transform(real_part, imag_part, direction):
    total = real_part.shape[0]
    channels = real_part.shape[1]
    inner = total // first_radix
    real_grid = real_part.reshape(inner, first_radix, channels)
    imag_grid = imag_part.reshape(inner, first_radix, channels)
    cos_inner, sin_inner = twiddles(inner, inner, inner, direction)
    step_real = jnp.einsum("kn,nac->kac", cos_inner, real_grid, precision=highest) - jnp.einsum(
        "kn,nac->kac", sin_inner, imag_grid, precision=highest
    )
    step_imag = jnp.einsum("kn,nac->kac", cos_inner, imag_grid, precision=highest) + jnp.einsum(
        "kn,nac->kac", sin_inner, real_grid, precision=highest
    )
    cos_twist, sin_twist = twiddles(inner, first_radix, total, direction)
    cos_twist = cos_twist[:, :, None]
    sin_twist = sin_twist[:, :, None]
    twist_real = step_real * cos_twist - step_imag * sin_twist
    twist_imag = step_real * sin_twist + step_imag * cos_twist
    cos_outer, sin_outer = twiddles(first_radix, first_radix, first_radix, direction)
    out_real = jnp.einsum("jn,knc->jkc", cos_outer, twist_real, precision=highest) - jnp.einsum(
        "jn,knc->jkc", sin_outer, twist_imag, precision=highest
    )
    out_imag = jnp.einsum("jn,knc->jkc", cos_outer, twist_imag, precision=highest) + jnp.einsum(
        "jn,knc->jkc", sin_outer, twist_real, precision=highest
    )
    return (out_real.reshape(total, channels), out_imag.reshape(total, channels))


def mirror(values):
    return jnp.roll(jnp.flip(values, 0), 1, 0)


def split_spectra(real_signal):
    half = real_signal.shape[1] // 2
    padded = jnp.concatenate([real_signal, jnp.zeros_like(real_signal)], axis=0)
    whole_real, whole_imag = transform(padded[:, :half], padded[:, half:], -1.0)
    back_real = mirror(whole_real)
    back_imag = mirror(whole_imag)
    first_real = 0.5 * (whole_real + back_real)
    first_imag = 0.5 * (whole_imag - back_imag)
    second_real = 0.5 * (whole_imag + back_imag)
    second_imag = 0.5 * (back_real - whole_real)
    return (first_real, first_imag, second_real, second_imag)


def kernel_spectra(long_taps):
    position = lax.broadcasted_iota(jnp.float32, (long_taps.shape[0], 1), 0)
    return split_spectra(long_taps * jnp.exp(-decay_rate * position))


def causal_conv(signal, spectra):
    length = signal.shape[0]
    sig_a_real, sig_a_imag, sig_b_real, sig_b_imag = split_spectra(signal)
    ker_a_real, ker_a_imag, ker_b_real, ker_b_imag = spectra
    first_real = sig_a_real * ker_a_real - sig_a_imag * ker_a_imag
    first_imag = sig_a_real * ker_a_imag + sig_a_imag * ker_a_real
    second_real = sig_b_real * ker_b_real - sig_b_imag * ker_b_imag
    second_imag = sig_b_real * ker_b_imag + sig_b_imag * ker_b_real
    out_real, out_imag = transform(first_real - second_imag, first_imag + second_real, 1.0)
    scale = 1.0 / (2 * length)
    return jnp.concatenate([out_real[:length], out_imag[:length]], axis=1) * scale


def short_conv(values, short_taps):
    length = values.shape[0]
    padded = jnp.pad(values, ((2, 0), (0, 0)))
    return (
        short_taps[0] * padded[2:]
        + short_taps[1] * padded[1 : length + 1]
        + short_taps[2] * padded[:length]
    )


def conv_part(mixed, short_taps, spectra):
    smooth = short_conv(mixed, short_taps)
    width = smooth.shape[1] // 3
    query = smooth[:, :width]
    key_part = smooth[:, width : 2 * width]
    value_part = smooth[:, 2 * width :]
    return query * causal_conv(key_part * value_part, spectra)


def pack_shards(pieces, total):
    flat = jnp.concatenate([piece.reshape(-1) for piece in pieces])
    return jnp.pad(flat, (0, total - flat.shape[0]))


def unpack_shards(flat, layout):
    pieces = []
    offset = 0
    for shape, split_dim in layout:
        count = math.prod(shape)
        pieces.append(flat[offset : offset + count].reshape(shape))
        offset += count
    return tuple(pieces)


def unpack_whole(flat, layout, chans, total):
    grid = flat.reshape(chans, total)
    pieces = []
    offset = 0
    for shape, split_dim in layout:
        count = math.prod(shape)
        block = grid[:, offset : offset + count].reshape((chans,) + shape)
        block = jnp.moveaxis(block, 0, split_dim)
        whole_shape = tuple(
            (
                size_one * chans if axis_id == split_dim else size_one
                for axis_id, size_one in enumerate(shape)
            )
        )
        pieces.append(block.reshape(whole_shape))
        offset += count
    return tuple(pieces)


def pack_whole(pieces, layout, chans, total):
    rows = []
    for piece, (shape, split_dim) in zip(pieces, layout):
        split_shape = shape[:split_dim] + (chans,) + shape[split_dim:]
        block = jnp.moveaxis(piece.reshape(split_shape), split_dim, 0)
        rows.append(block.reshape(chans, -1))
    grid = jnp.concatenate(rows, axis=1)
    grid = jnp.pad(grid, ((0, 0), (0, total - grid.shape[1])))
    return grid.reshape(-1)


def body(
    inputs,
    lengths,
    out_grad,
    ln_mix_gain,
    w_in,
    short_taps,
    long_taps,
    w_out,
    ln_mlp_gain,
    w_up,
    w_down,
):
    segments = lax.axis_size("section")
    chans = lax.axis_size("chan")
    segment = lax.axis_index("section")
    layer = segment // 2
    is_mixer = segment % 2 == 0
    layer_count = ln_mix_gain.shape[0]
    part_d = D // chans
    part_ff = FF // chans
    tap_rows = long_taps.shape[1]
    mixer_layout = (
        ((part_d,), 0),
        ((part_d, 3 * D), 0),
        ((3, 3 * D // chans), 1),
        ((tap_rows, part_d), 1),
        ((part_d, D), 0),
    )
    mlp_layout = (((part_d,), 0), ((part_d, FF), 0), ((part_ff, D), 0))
    total = part_d * max(10 + 4 * D + tap_rows, 1 + 2 * FF)
    picked = tuple(
        (
            lax.dynamic_index_in_dim(weight, layer, 0, keepdims=False)
            for weight in (
                ln_mix_gain,
                w_in,
                short_taps,
                long_taps,
                w_out,
                ln_mlp_gain,
                w_up,
                w_down,
            )
        )
    )
    mixer_local = pack_shards(picked[:5], total)
    mlp_local = pack_shards(picked[5:], total)
    own_local = jnp.where(is_mixer, mixer_local, mlp_local)
    gathered = lax.all_gather(own_local, "chan", axis=0, tiled=True)
    mixer_full = unpack_whole(gathered, mixer_layout, chans, total)
    mlp_full = unpack_whole(gathered, mlp_layout, chans, total)
    gain_mix = mixer_full[0].astype(jnp.float32)
    proj_in = mixer_full[1]
    short_full = mixer_full[2].astype(jnp.float32)
    taps_full = mixer_full[3].astype(jnp.float32)
    proj_out = mixer_full[4]
    gain_mlp = mlp_full[0].astype(jnp.float32)
    proj_up = mlp_full[1]
    proj_down = mlp_full[2]
    spectra, spectra_pull = jax.vjp(kernel_spectra, taps_full)
    micro = inputs.shape[0]
    length = inputs.shape[2]
    local_inputs = inputs[:, 0]
    local_cotangent = out_grad[:, 0]
    position = lax.broadcasted_iota(jnp.int32, (length, 1), 0)
    packed_zero = jnp.zeros((chans * total,), jnp.float32)

    def live_of(index):
        return (position < lengths[index, 0]).astype(jnp.float32)

    def spare_forward(values, live_mask):
        return jnp.zeros(values.shape, jnp.float32)

    def mixer_forward(values, live_mask):
        floats = values.astype(jnp.float32)
        normed = layer_norm(floats, gain_mix).astype(jnp.bfloat16)
        mixed = jnp.dot(normed, proj_in, preferred_element_type=jnp.float32)
        gated = conv_part(mixed, short_full, spectra).astype(jnp.bfloat16)
        branch = jnp.dot(gated, proj_out, preferred_element_type=jnp.float32)
        return live_mask * (floats + branch)

    def mlp_forward(values, live_mask):
        floats = values.astype(jnp.float32)
        normed = layer_norm(floats, gain_mlp).astype(jnp.bfloat16)
        pre_act = jnp.dot(normed, proj_up, preferred_element_type=jnp.float32)
        hidden = jax.nn.gelu(pre_act, approximate=False).astype(jnp.bfloat16)
        branch = jnp.dot(hidden, proj_down, preferred_element_type=jnp.float32)
        return live_mask * (floats + branch)

    def spare_backward(values, upstream, live_mask):
        return (jnp.zeros(values.shape, jnp.float32), packed_zero)

    def mixer_backward(values, upstream, live_mask):
        floats = values.astype(jnp.float32)
        masked = live_mask * upstream
        normed_float, norm_pull = jax.vjp(layer_norm, floats, gain_mix)
        normed = normed_float.astype(jnp.bfloat16)
        mixed = jnp.dot(normed, proj_in, preferred_element_type=jnp.float32)
        gated_float, conv_pull = jax.vjp(conv_part, mixed, short_full, spectra)
        gated = gated_float.astype(jnp.bfloat16)
        branch_grad = masked.astype(jnp.bfloat16)
        grad_out = jnp.einsum("ti,to->io", gated, branch_grad, preferred_element_type=jnp.float32)
        grad_gated = jnp.einsum(
            "to,io->ti", branch_grad, proj_out, preferred_element_type=jnp.float32
        )
        grad_mixed, grad_short, grad_spectra = conv_pull(grad_gated)
        (grad_taps,) = spectra_pull(grad_spectra)
        mixed_grad = grad_mixed.astype(jnp.bfloat16)
        grad_in = jnp.einsum("ti,tj->ij", normed, mixed_grad, preferred_element_type=jnp.float32)
        grad_normed = jnp.einsum(
            "tj,ij->ti", mixed_grad, proj_in, preferred_element_type=jnp.float32
        )
        grad_values, grad_gain = norm_pull(grad_normed)
        packed = pack_whole(
            (grad_gain, grad_in, grad_short, grad_taps, grad_out), mixer_layout, chans, total
        )
        return (masked + grad_values, packed)

    def mlp_backward(values, upstream, live_mask):
        floats = values.astype(jnp.float32)
        masked = live_mask * upstream
        normed_float, norm_pull = jax.vjp(layer_norm, floats, gain_mlp)
        normed = normed_float.astype(jnp.bfloat16)
        pre_act = jnp.dot(normed, proj_up, preferred_element_type=jnp.float32)
        hidden_float, gelu_pull = jax.vjp(
            lambda pre_value: jax.nn.gelu(pre_value, approximate=False), pre_act
        )
        hidden = hidden_float.astype(jnp.bfloat16)
        branch_grad = masked.astype(jnp.bfloat16)
        grad_down = jnp.einsum("tf,to->fo", hidden, branch_grad, preferred_element_type=jnp.float32)
        grad_hidden = jnp.einsum(
            "to,fo->tf", branch_grad, proj_down, preferred_element_type=jnp.float32
        )
        (grad_pre,) = gelu_pull(grad_hidden)
        pre_grad = grad_pre.astype(jnp.bfloat16)
        grad_up = jnp.einsum("ti,tf->if", normed, pre_grad, preferred_element_type=jnp.float32)
        grad_normed = jnp.einsum("tf,if->ti", pre_grad, proj_up, preferred_element_type=jnp.float32)
        grad_values, grad_gain = norm_pull(grad_normed)
        packed = pack_whole((grad_gain, grad_up, grad_down), mlp_layout, chans, total)
        return (masked + grad_values, packed)

    steps_total = micro + segments - 1

    def forward_step(step, carry):
        incoming, kept_inputs, sent_all = carry
        index = step - segment
        valid = (index >= 0) & (index < micro)
        safe = jnp.clip(index, 0, micro - 1)
        own_input = jnp.where(segment == 0, local_inputs[safe], incoming)
        branch_id = jnp.where(valid, 1 + segment % 2, 0)
        result = lax.switch(
            branch_id, (spare_forward, mixer_forward, mlp_forward), own_input, live_of(safe)
        )
        sent = result.astype(jnp.bfloat16)
        kept_inputs = lax.dynamic_update_index_in_dim(
            kept_inputs, jnp.where(valid, own_input, kept_inputs[safe]), safe, 0
        )
        sent_all = lax.dynamic_update_index_in_dim(
            sent_all, jnp.where(valid, sent, sent_all[safe]), safe, 0
        )
        incoming = from_behind(sent, "section", 1)
        return (incoming, kept_inputs, sent_all)

    blank_rows = jnp.zeros(local_inputs.shape[1:], jnp.bfloat16)
    blank_store = jnp.zeros(local_inputs.shape, jnp.bfloat16)
    unused_rows, kept_inputs, sent_all = lax.fori_loop(
        0, steps_total, forward_step, (blank_rows, blank_store, blank_store)
    )

    def backward_step(step, carry):
        incoming, input_grads, accum = carry
        index = step - (segments - 1 - segment)
        valid = (index >= 0) & (index < micro)
        safe = jnp.clip(index, 0, micro - 1)
        upstream = jnp.where(segment == segments - 1, local_cotangent[safe], incoming).astype(
            jnp.float32
        )
        branch_id = jnp.where(valid, 1 + segment % 2, 0)
        grad_values, packed = lax.switch(
            branch_id,
            (spare_backward, mixer_backward, mlp_backward),
            kept_inputs[safe],
            upstream,
            live_of(safe),
        )
        input_grads = lax.dynamic_update_index_in_dim(
            input_grads, jnp.where(valid, grad_values, input_grads[safe]), safe, 0
        )
        accum = accum + packed
        incoming = from_behind(grad_values.astype(jnp.bfloat16), "section", -1)
        return (incoming, input_grads, accum)

    grad_store = jnp.zeros(local_inputs.shape, jnp.float32)
    unused_grads, input_grads, accum = lax.fori_loop(
        0, steps_total, backward_step, (blank_rows, grad_store, packed_zero)
    )
    own_shard = lax.psum_scatter(
        accum.astype(jnp.bfloat16), "chan", scatter_dimension=0, tiled=True
    ).astype(jnp.float32)
    mixer_weight = is_mixer.astype(jnp.float32)
    mlp_weight = 1.0 - mixer_weight
    shards = tuple(
        (piece * mixer_weight for piece in unpack_shards(own_shard, mixer_layout))
    ) + tuple((piece * mlp_weight for piece in unpack_shards(own_shard, mlp_layout)))
    layer_hot = (lax.iota(jnp.int32, layer_count) == layer).astype(jnp.float32)
    placed = tuple(
        (layer_hot.reshape((layer_count,) + (1,) * piece.ndim) * piece[None] for piece in shards)
    )
    totals = (
        lax.psum(placed[0].astype(jnp.bfloat16), ("section", "dp")).astype(jnp.float32),
        lax.psum(placed[1].astype(jnp.bfloat16), ("section", "dp")).astype(jnp.float32),
        lax.psum(placed[2].astype(jnp.bfloat16), ("section", "dp")).astype(jnp.float32),
        lax.psum(placed[3].astype(jnp.bfloat16), ("section", "dp")).astype(jnp.float32),
        lax.psum(placed[4].astype(jnp.bfloat16), ("section", "dp")).astype(jnp.float32),
        lax.psum(placed[5].astype(jnp.bfloat16), ("section", "dp")).astype(jnp.float32),
        lax.psum(placed[6].astype(jnp.bfloat16), ("section", "dp")).astype(jnp.float32),
        lax.psum(placed[7].astype(jnp.bfloat16), ("section", "dp")).astype(jnp.float32),
    )
    return (
        sent_all[None, :, None],
        input_grads[None, :, None],
        totals[0],
        totals[1],
        totals[2],
        totals[3],
        totals[4],
        totals[5],
        totals[6],
        totals[7],
    )


def solution(mesh):
    return jax.shard_map(
        body,
        mesh=mesh,
        in_specs=(
            P(None, ("dp", "chan"), None, None),
            P(None, ("dp", "chan")),
            P(None, ("dp", "chan"), None, None),
            P(None, "chan"),
            P(None, "chan", None),
            P(None, None, "chan"),
            P(None, None, "chan"),
            P(None, "chan", None),
            P(None, "chan"),
            P(None, "chan", None),
            P(None, "chan", None),
        ),
        out_specs=(
            P("section", None, ("dp", "chan"), None, None),
            P("section", None, ("dp", "chan"), None, None),
            P(None, "chan"),
            P(None, "chan", None),
            P(None, None, "chan"),
            P(None, None, "chan"),
            P(None, "chan", None),
            P(None, "chan"),
            P(None, "chan", None),
            P(None, "chan", None),
        ),
        check_vma=False,
    )
```

profile of v0, /device:TPU:0, one launch (start us, length us, event | category | flops | bytes accessed | tf_op | source)
XLA Modules:
  0.0 3358.4 jit_solution(15341648354509061815)
XLA Ops:
  17.9 26.5 concatenate.48
  44.4 28.4 concatenate.47
  80.7 36.5 %dynamic-update-slice = bf16[4719360]{0:T(1024)(128)(2,1)} dynamic-update-slice(bf16[4719360]{0:T(1024)(128)(2,1)} %broadcast.906, bf16[1179840]{0:T(1024)(128)(2,1)S(1)} %copy-done.50, u32[]{:T(128)} %bitcast.89) | dynamic-update-slice | bytes 4719364
  122.1 323.3 %all-reduce.38.cloned.1.call-done = bf16[4719360]{0:T(1024)(128)(2,1)} async-done(((bf16[4719360]{0:T(1024)(128)(2,1)}), bf16[4719360]{0:T(1024)(128)(2,1)}) %all-reduce.38.cloned.1.call-update) | async-done | bytes 9438736
  561.4 25.6 slice.218
  629.2 456.2 %while.45 = (s32[]{:T(128)}, bf16[1024,768]{1,0:T(8,128)(2,1)}, bf16[2,1024,768]{2,1,0:T(8,128)(2,1)}, bf16[2,1024,768]{2,1,0:T(8,128)(2,1)}, s32[]{:T(128)}, /*...) while((s32[]{:T(128)}, bf16[1024,768]{1,0:T(8,128)(2,1)}, ...), condition=%wide.region_8.9_spmd.clone, body=%wide.region_0.8_spmd.clone.sunk | while | flops 12143930368 | bytes 445312256 | solution.py:330
  636.2 180.6 %conditional.7 = (bf16[1024,768]{1,0:T(8,128)(2,1)S(1)}) conditional(s32[]{:T(128)} %clamp.27, () %tuple.229, (f32[1024,1]{0,1:T(1,128)S(1)}, bf16[1024,768]{1,0:T(8,128)(2,1)S(1)}, f32[3,2304]{1,0:T(4,128)S(1)}, f32[768]{0:T(1024)S(1)}, bf16[768,2304]{1,0:T(8,128)(2,1)}, /*index=5*/f32[2048,384]{1,0:T(8,128)}, ...), branch_computations={%region_1.1_spmd, %region_2.4_spmd, %region_5.7_spmd} | conditional | flops 12141569024 | bytes 388684000 | solution.py:315
  685.7 25.5 slice.163
  830.4 180.6 %conditional.7 = (bf16[1024,768]{1,0:T(8,128)(2,1)S(1)}) conditional(s32[]{:T(128)} %clamp.27, () %tuple.229, (f32[1024,1]{0,1:T(1,128)S(1)}, bf16[1024,768]{1,0:T(8,128)(2,1)S(1)}, f32[3,2304]{1,0:T(4,128)S(1)}, f32[768]{0:T(1024)S(1)}, bf16[768,2304]{1,0:T(8,128)(2,1)}, /*index=5*/f32[2048,384]{1,0:T(8,128)}, ...), branch_computations={%region_1.1_spmd, %region_2.4_spmd, %region_5.7_spmd} | conditional | flops 12141569024 | bytes 388684000 | solution.py:315
  1027.8 51.0 %collective-permute-start = (bf16[1024,768]{1,0:T(8,128)(2,1)S(1)}, bf16[1024,768]{1,0:T(8,128)(2,1)S(1)}, u32[]{:S(2)}, u32[]{:S(2)}) collective-permute-start(bf16[1024,768]{1,0:T(8,128)(2,1)S(1)} %get-tuple-element.2684), channel_id=1, source_target_pairs={{0,16},{1,17},{2,18},{3,19},{4,20},{5,21},{6,22},{7,23},{8,24},{9,... | collective-permute-start | bytes 4718600 | tf_op jit(solution)/shard_map/while/body/eval_jaxpr/ppermute | solution.py:20
  1089.9 1821.9 %while.46 = (s32[]{:T(128)}, bf16[1024,768]{0,1:T(8,128)(2,1)}, f32[2,1024,768]{2,1,0:T(8,128)}, f32[4719360]{0:T(1024)}, s32[]{:T(128)}, /*index=5*/s32[]{:T(12...) while((s32[]{:T(128)}, bf16[1024,768]{0,1:T(8,128)(2,1)}, ...), condition=%wide.region_26.27_spmd.clone.clone, body=%wide.region_9.26_spmd.clone.clone.sunk | while | flops 31621392384 | bytes 1710592256 | solution.py:358
  1145.3 260.8 %collective-permute-done.1 = bf16[1024,768]{0,1:T(8,128)(2,1)} collective-permute-done((bf16[1024,768]{0,1:T(8,128)(2,1)}, bf16[1024,768]{0,1:T(8,128)(2,1)}, u32[]{:S(2)}, u32[]{:S(2)}) %collective-permute-start.1) | collective-permute-done | bytes 1572896 | tf_op jit(solution)/shard_map/while/body/eval_jaxpr/ppermute | solution.py:20
  1421.1 702.8 %conditional.8 = (f32[1024,768]{0,1:T(8,128)}, f32[4719360]{0:T(1024)}) conditional(s32[]{:T(128)} %clamp.28, () %tuple.234, (f32[1024,1]{0,1:T(1,128)S(1)}, f32[1024,768]{0,1:T(8,128)S(1)}, f32[3,2304]{1,0:T(4,128)}, bf16[1024,768]{0,1:T(8,128)(2,1)S(1)}, f32[768]{0:T(1024)S(1)}, ...), branch_computations={%region_10.10_spmd, %region_11.19_spmd.clone, %region_20.25_spmd} | conditional | flops 31608705024 | bytes 1579752064 | solution.py:343
  1468.8 25.7 slice.247
  1511.1 26.0 slice.244
  1983.9 37.6 %dynamic-update-slice.5 = f32[4,788352]{1,0:T(4,128)} dynamic-update-slice(f32[4,788352]{1,0:T(4,128)} %dynamic-update-slice.4, f32[4,442368]{1,0:T(4,128)} %reshape.695, s32[]{} %constant.653, s32[]{} %constant.654) | dynamic-update-slice | bytes 14155780 | tf_op jit(solution)/shard_map/while/body/eval_jaxpr/cond
  2051.8 56.4 %reshape.703 = f32[4719360]{0:T(1024)} reshape(f32[4,1179840]{1,0:T(4,128)} %pad.121) | data formatting | bytes 37754880 | tf_op jit(solution)/shard_map/while/body/eval_jaxpr/cond/branch_1_fun/reshape | solution.py:161
  2171.4 702.8 %conditional.8 = (f32[1024,768]{0,1:T(8,128)}, f32[4719360]{0:T(1024)}) conditional(s32[]{:T(128)} %clamp.28, () %tuple.234, (f32[1024,1]{0,1:T(1,128)S(1)}, f32[1024,768]{0,1:T(8,128)S(1)}, f32[3,2304]{1,0:T(4,128)}, bf16[1024,768]{0,1:T(8,128)(2,1)S(1)}, f32[768]{0:T(1024)S(1)}, ...), branch_computations={%region_10.10_spmd, %region_11.19_spmd.clone, %region_20.25_spmd} | conditional | flops 31608705024 | bytes 1579752064 | solution.py:343
  2219.1 25.7 slice.247
  2261.4 26.0 slice.244
  2734.2 37.6 %dynamic-update-slice.5 = f32[4,788352]{1,0:T(4,128)} dynamic-update-slice(f32[4,788352]{1,0:T(4,128)} %dynamic-update-slice.4, f32[4,442368]{1,0:T(4,128)} %reshape.695, s32[]{} %constant.653, s32[]{} %constant.654) | dynamic-update-slice | bytes 14155780 | tf_op jit(solution)/shard_map/while/body/eval_jaxpr/cond
  2802.1 56.4 %reshape.703 = f32[4719360]{0:T(1024)} reshape(f32[4,1179840]{1,0:T(4,128)} %pad.121) | data formatting | bytes 37754880 | tf_op jit(solution)/shard_map/while/body/eval_jaxpr/cond/branch_1_fun/reshape | solution.py:161
  2923.8 325.9 %all-reduce.40.cloned.1.call-done = bf16[4719360]{0:T(1024)(128)(2,1)} async-done(((bf16[4719360]{0:T(1024)(128)(2,1)}), bf16[4719360]{0:T(1024)(128)(2,1)}) %all-reduce.40.cloned.1.call-update) | async-done | bytes 9438736
  3283.0 60.6 %all-reduce.42.cloned.1.call-done = (bf16[1,1024,192]{2,1,0:T(8,128)(2,1)}, bf16[1,192,2304]{2,1,0:T(8,128)(2,1)}, bf16[1,192,768]{2,1,0:T(8,128)(2,1)}, bf16[1,...) async-done(((bf16[1,1024,192]{2,1,0:T(8,128)(2,1)}, bf16[1,192,2304]{2,1,0:T(8,128)(2,1)}, bf16[1,192,768]{2,1,0:T(8,128)(2,1)}, bf16[1,192,3072]{2,1,0:T(8,128)(2,1)}, ...) | async-done | bytes 3932176 | tf_op jit(solution)/shard_map/psum | solution.py:377
  (905 shorter events, 1846.3 us)
Async XLA Ops:
  7.2 438.2 %all-reduce.38.cloned.1.call-start = ((), (), s32[]{:S(2)}) async-start(), calls=%async_computation | async-start | bytes 18878464
  117.2 3132.5 %all-reduce.40.cloned.1.call-start = ((), (), s32[]{:S(2)}) async-start(), calls=%async_computation.1 | async-start | bytes 18878464
  816.8 4.3 collective-permute-start
  1011.0 4.3 collective-permute-start
  1027.8 54.0 %collective-permute-start = (bf16[1024,768]{1,0:T(8,128)(2,1)S(1)}, bf16[1024,768]{1,0:T(8,128)(2,1)S(1)}, u32[]{:S(2)}, u32[]{:S(2)}) collective-permute-start(bf16[1024,768]{1,0:T(8,128)(2,1)S(1)} %get-tuple-element.2684), channel_id=1, source_target_pairs={{0,16},{1,17},{2,18},{3,19},{4,20},{5,21},{6,22},{7,23},{8,24},{9,... | collective-permute-start | bytes 4718600 | tf_op jit(solution)/shard_map/while/body/eval_jaxpr/ppermute | solution.py:20
  1092.2 14.3 copy-start.74
  1124.8 281.2 %collective-permute-start.1 = (bf16[1024,768]{0,1:T(8,128)(2,1)}, bf16[1024,768]{0,1:T(8,128)(2,1)}, u32[]{:S(2)}, u32[]{:S(2)}) collective-permute-start(bf16[1024,768]{0,1:T(8,128)(2,1)} %get-tuple-element.2535), channel_id=1, source_target_pairs={{16,0},{17,1},{18,2},{19,3},{20,4},{21,5},{22,6},{23,7},{24,8},{25... | collective-permute-start | bytes 4718600 | tf_op jit(solution)/shard_map/while/body/eval_jaxpr/ppermute | solution.py:20
  1143.4 262.7 %copy-start.72 = (f32[3,2304]{1,0:T(4,128)S(1)}, f32[3,2304]{1,0:T(4,128)}, u32[]{:S(2)}) copy-start(f32[3,2304]{1,0:T(4,128)} %copy-done.71) | copy-start | bytes 82948 | tf_op jit(solution)/shard_map/while
  1143.4 262.7 %copy-start.75 = (f32[768]{0:T(1024)S(1)}, f32[768]{0:T(1024)}, u32[]{:S(2)}) copy-start(f32[768]{0:T(1024)} %copy-done.74) | copy-start | bytes 9220 | tf_op jit(solution)/shard_map/while
  1406.8 14.3 copy-start.74
  1581.7 11.6 copy-start.11
  1593.4 10.9 copy-start.13
  1606.4 24.9 copy-start.35
  1862.7 11.9 slice-start
  1947.2 10.7 copy-start.63
  2131.0 25.2 collective-permute-start.1
  2157.1 14.3 copy-start.74
  2332.0 11.6 copy-start.11
  2343.7 10.9 copy-start.13
  2356.7 24.9 copy-start.35
  2613.0 11.9 slice-start
  2697.5 10.7 copy-start.63
  2881.3 25.2 collective-permute-start.1
  2923.1 420.6 %all-reduce.42.cloned.1.call-start = ((), (), s32[]{:S(2)}) async-start(), calls=%async_computation.2 | async-start | bytes 8126464 | tf_op jit(solution)/shard_map/psum | solution.py:377
  (177 other events, 767.1 us)
Sparse Core Ops, SparseCore 0:
  117.4 327.9 all-reduce.37
  2923.2 326.5 all-reduce.39
  3262.9 80.6 all-reduce.41
where the time goes:
time: 3400 us; the launch traced here: 3360 us
  local copies, waits for them, and re-layouts  1140 us (34%)
  waiting for transfers between devices  971 us (29%)
  matrix products  684 us (20%)
  other arithmetic  415 us (12%)
  starting transfers between devices  58.3 us (2%)
  loops' own time  54.9 us (2%)
    unnamed x5, waiting for transfers between devices  649 us
    slice x30, local copies, waits for them, and re-layouts, mirror(): return jnp.roll(jnp.flip(values, 0), 1, 0)  268 us
    ppermute x6, waiting for transfers between devices, from_behind(): lax.ppermute(value, axis, [(source, source + steps) for source in range(i...  261 us
    rev x8, local copies, waits for them, and re-layouts, mirror(): return jnp.roll(jnp.flip(values, 0), 1, 0)  199 us
    cond x284, local copies, waits for them, and re-layouts  128 us
    reshape x2, local copies, waits for them, and re-layouts, pack_whole(): return grid.reshape(-1)  113 us
    dot_general x15, matrix products, transform(): jnp.einsum('kn,nac->kac', sin_inner, real_grid, precision=highest)  79.9 us
    dot_general x15, matrix products, transform(): jnp.einsum('jn,knc->jkc', sin_outer, twist_real, precision=highest)  79.9 us
  transfers between devices with their start and end apart: 9, of which 4 were waited for; matrix products, arithmetic and copies ran while one was open for 2% of the time, Pallas kernels for 0%

commit v1 on v0

v1 whole, which is shorter than its diff:
```python
import math

import jax
import jax.numpy as jnp
import ml_dtypes
import numpy as np
from jax import lax
from jax.sharding import PartitionSpec as P

D = 768
FF = 3072
decay_rate = 0.003
bf16 = jnp.bfloat16
f32 = jnp.float32


def odd_basis(length):
    phase = (2 * np.arange(length)[:, None] + 1) * np.arange(length)[None, :] % (4 * length)
    angle = phase * (math.pi / (2 * length))
    return np.concatenate([np.cos(angle), np.sin(angle)], 0).astype(ml_dtypes.bfloat16)


def dot(a, b, ca=1, cb=0):
    return lax.dot_general(a, b, (((ca,), (cb,)), ((), ())), preferred_element_type=f32)


def shift_down(v, n):
    return jnp.pad(v, ((n, 0), (0, 0)))[: v.shape[0]]


def shift_up(v, n):
    return jnp.pad(v, ((0, n), (0, 0)))[n:]


def norm_parts(values):
    centered = values - jnp.mean(values, axis=-1, keepdims=True)
    spread = jnp.mean(centered * centered, axis=-1, keepdims=True)
    inv = lax.rsqrt(spread + 1e-05)
    return centered * inv, inv


def norm_back(grad_normed, hat, inv, gain):
    grad_hat = grad_normed * gain
    return inv * (
        grad_hat
        - jnp.mean(grad_hat, axis=-1, keepdims=True)
        - hat * jnp.mean(grad_hat * hat, axis=-1, keepdims=True)
    )


def body(inputs, lengths, out_grad, ln_mix_gain, w_in, short_taps, long_taps, w_out, ln_mlp_gain, w_up, w_down):
    chans = lax.axis_size("chan")
    own = lax.axis_index("section")
    length = inputs.shape[2]
    position = lax.broadcasted_iota(jnp.int32, (length, 1), 0)
    x = lax.dynamic_index_in_dim(inputs[:, 0], own, 0, keepdims=False).astype(f32)
    og = lax.dynamic_index_in_dim(out_grad[:, 0], own, 0, keepdims=False)
    live = (position < lax.dynamic_index_in_dim(lengths[:, 0], own, 0, keepdims=False)).astype(f32)

    def rows(w):
        return lax.all_gather(w[0], "chan", axis=0, tiled=True)

    def cols(w):
        return lax.all_gather(w[0], "chan", axis=1, tiled=True)

    gain_mix = cols(ln_mix_gain[None])[0].astype(f32)
    gain_mlp = cols(ln_mlp_gain[None])[0].astype(f32)
    taps = cols(short_taps).astype(f32)
    kern = cols(long_taps).astype(f32)
    proj_in, proj_out, proj_up, proj_down = rows(w_in), rows(w_out), rows(w_up), rows(w_down)

    basis = jnp.asarray(odd_basis(length))
    decay = jnp.exp(-decay_rate * position.astype(f32))
    half = length

    def spectrum(v):
        both = dot(basis, v)
        return both[:half], both[half:]

    def back(cos_part, sin_part):
        return dot(basis, jnp.concatenate([cos_part, sin_part], 0).astype(bf16), 0, 0)

    kc, ks = spectrum((kern * decay).astype(bf16))
    kc, ks = kc / length, ks / length
    hat0, inv0 = norm_parts(x)
    normed0 = (hat0 * gain_mix).astype(bf16)
    mixed = dot(normed0, proj_in)
    smooth = taps[0] * mixed + taps[1] * shift_down(mixed, 1) + taps[2] * shift_down(mixed, 2)
    query, key, value = smooth[:, :D], smooth[:, D : 2 * D], smooth[:, 2 * D :]
    sc, ss = spectrum((key * value).astype(bf16))
    conv = back(sc * kc - ss * ks, sc * ks + ss * kc)
    gated = (query * conv).astype(bf16)
    act0 = (live * (x + dot(gated, proj_out))).astype(bf16)
    x1 = act0.astype(f32)
    hat1, inv1 = norm_parts(x1)
    normed1 = (hat1 * gain_mlp).astype(bf16)
    pre = dot(normed1, proj_up)
    cdf = 0.5 * (1.0 + lax.erf(pre * math.sqrt(0.5)))
    hidden = (pre * cdf).astype(bf16)
    act1 = (live * (x1 + dot(hidden, proj_down))).astype(bf16)
    masked1 = live * og.astype(f32)
    branch1 = masked1.astype(bf16)
    g_down = dot(hidden, branch1, 0, 0)
    slope = cdf + pre * (jnp.exp(-0.5 * pre * pre) * (1.0 / math.sqrt(2.0 * math.pi)))
    pre_grad = (slope * dot(branch1, proj_down, 1, 1)).astype(bf16)
    g_up = dot(normed1, pre_grad, 0, 0)
    gn1 = dot(pre_grad, proj_up, 1, 1)
    g_gain_mlp = jnp.sum(gn1 * hat1, axis=0)
    ag1 = masked1 + norm_back(gn1, hat1, inv1, gain_mlp)
    ag1_low = ag1.astype(bf16)
    masked0 = live * ag1_low.astype(f32)
    branch0 = masked0.astype(bf16)
    g_out = dot(gated, branch0, 0, 0)
    grad_gated = dot(branch0, proj_out, 1, 1)
    gc, gs = spectrum((grad_gated * query).astype(bf16))
    g_kern = back(sc * gc + ss * gs, sc * gs - ss * gc) * (decay / length)
    g_sig = back(kc * gc + ks * gs, kc * gs - ks * gc)
    g_smooth = jnp.concatenate([grad_gated * conv, g_sig * value, g_sig * key], 1)
    g_taps = jnp.stack([jnp.sum(g_smooth * shift_down(mixed, n), axis=0) if n else jnp.sum(g_smooth * mixed, axis=0) for n in range(3)])
    g_mixed = (taps[0] * g_smooth + taps[1] * shift_up(g_smooth, 1) + taps[2] * shift_up(g_smooth, 2)).astype(bf16)
    g_in = dot(normed0, g_mixed, 0, 0)
    gn0 = dot(g_mixed, proj_in, 1, 1)
    g_gain_mix = jnp.sum(gn0 * hat0, axis=0)
    ag0 = masked0 + norm_back(gn0, hat0, inv0, gain_mix)

    swap = [(0, 1), (1, 0)]
    first = own == 0

    def exchange(own_first, own_second, dtype):
        keep = jnp.where(first, own_first, own_second).astype(dtype)
        other = lax.ppermute(jnp.where(first, own_second, own_first).astype(bf16), "section", swap).astype(dtype)
        both = jnp.stack([jnp.where(first, keep, other), jnp.where(first, other, keep)])
        return both[None, :, None]

    def reduced(g, dim):
        part = lax.psum_scatter(g.astype(bf16), "chan", scatter_dimension=dim, tiled=True)
        return lax.psum(part, ("section", "dp")).astype(f32)[None]

    return (
        exchange(act0, act1, bf16),
        exchange(ag0, ag1, f32),
        reduced(g_gain_mix, 0),
        reduced(g_in, 0),
        reduced(g_taps, 1),
        reduced(g_kern, 1),
        reduced(g_out, 0),
        reduced(g_gain_mlp, 0),
        reduced(g_up, 0),
        reduced(g_down, 0),
    )


def solution(mesh):
    return jax.shard_map(
        body,
        mesh=mesh,
        in_specs=(
            P(None, ("dp", "chan"), None, None),
            P(None, ("dp", "chan")),
            P(None, ("dp", "chan"), None, None),
            P(None, "chan"),
            P(None, "chan", None),
            P(None, None, "chan"),
            P(None, None, "chan"),
            P(None, "chan", None),
            P(None, "chan"),
            P(None, "chan", None),
            P(None, "chan", None),
        ),
        out_specs=(
            P("section", None, ("dp", "chan"), None, None),
            P("section", None, ("dp", "chan"), None, None),
            P(None, "chan"),
            P(None, "chan", None),
            P(None, None, "chan"),
            P(None, None, "chan"),
            P(None, "chan", None),
            P(None, "chan"),
            P(None, "chan", None),
            P(None, "chan", None),
        ),
        check_vma=False,
    )
```

time: 3400 us -> 817 us (0.24); the launches traced: 3360 us -> 814 us
  local copies, waits for them, and re-layouts: 1140 us -> 92.3 us
  waiting for transfers between devices: 971 us -> 415 us
  matrix products: 684 us -> 163 us
  other arithmetic: 415 us -> 48.4 us
  blocking collectives: 16.9 us -> 78.6 us
  starting transfers between devices: 58.3 us -> 1.29 us
  loops' own time: 54.9 us -> 0 us
    unnamed x5 -> x13, waiting for transfers between devices: 649 us -> 16.8 us
    dot_general x134 -> x21, matrix products: 684 us -> 163 us  [dot(): lax.dot_general(a, b, (((ca,), (cb,)), ((), ())), preferred_element_type=...]
    ppermute x6 -> x2, waiting for transfers between devices: 261 us -> 0.01 us  [exchange(): lax.ppermute(jnp.where(first, own_second, own_first).astype(bf16), 'secti...]
    slice x53 -> x1, local copies, waits for them, and re-layouts: 293 us -> 68.9 us  [body(): taps[0] * mixed + taps[1] * shift_down(mixed, 1)]
    reduce_scatter x0 -> x5, waiting for transfers between devices: none -> 211 us  [reduced(): lax.psum_scatter(g.astype(bf16), 'chan', scatter_dimension=dim, tiled=True)]
    rev x8 -> x0, local copies, waits for them, and re-layouts: 199 us -> none  [mirror(): return jnp.roll(jnp.flip(values, 0), 1, 0)]
    reshape x26 -> x0, local copies, waits for them, and re-layouts: 179 us -> none  [the longest x2 113 us: pack_whole(): return grid.reshape(-1)]
    all_gather x0 -> x5, waiting for transfers between devices: none -> 144 us  [the longest x4 144 us: rows(): return lax.all_gather(w[0], 'chan', axis=0, tiled=True)]
  transfers between devices with their start and end apart: 9 -> 14, of which waited for: 4 -> 7; matrix products, arithmetic and copies ran while one was open for 2% -> 31% of each run, Pallas kernels for 0% -> 0%
where the time goes in v1:
time: 817 us; the launch traced here: 814 us
  waiting for transfers between devices  415 us (51%)
  matrix products  163 us (20%)
  local copies, waits for them, and re-layouts  92.3 us (11%)
  blocking collectives  78.6 us (10%)
  other arithmetic  48.4 us (6%)
  between operations  16.4 us (2%)
    reduce_scatter x5, waiting for transfers between devices, reduced(): lax.psum_scatter(g.astype(bf16), 'chan', scatter_dimension=dim, tiled=True)  211 us
    dot_general x21, matrix products, dot(): lax.dot_general(a, b, (((ca,), (cb,)), ((), ())), preferred_element_type=...  163 us
    all_gather x4, waiting for transfers between devices, rows(): return lax.all_gather(w[0], 'chan', axis=0, tiled=True)  144 us
    slice x1, local copies, waits for them, and re-layouts, body(): taps[0] * mixed + taps[1] * shift_down(mixed, 1)  68.9 us
    psum x1, waiting for transfers between devices, reduced(): return lax.psum(part, ('section', 'dp')).astype(f32)[None]  43.5 us
    all_gather x1, blocking collectives, cols(): return lax.all_gather(w[0], 'chan', axis=1, tiled=True)  38.2 us
    unnamed x2, blocking collectives  24.8 us
    unnamed x89, local copies, waits for them, and re-layouts  21.4 us
  transfers between devices with their start and end apart: 14, of which 7 were waited for; matrix products, arithmetic and copies ran while one was open for 31% of the time, Pallas kernels for 0%

profile of v1, /device:TPU:0, one launch (start us, length us, event | category | flops | bytes accessed | tf_op | source)
XLA Modules:
  0.0 814.3 jit_solution(15898564932826986878)
XLA Ops:
  16.3 13.8 %all-reduce.11 = (bf16[768]{0:T(1024)(128)(2,1)S(1)}, bf16[768]{0:T(1024)(128)(2,1)S(1)}) all-reduce(bf16[768]{0:T(1024)(128)(2,1)S(1)} %dynamic-update-slice, bf16[768]{0:T(1024)(128)(2,1)S(1)} %dynamic-update-slice.1), channel_id=1, replica_groups=mesh['section'=2,'chan'=4,'dp'=4] {'chan'}, use_global_device_ids=true, to_apply=%add.4 | all-reduce | flops 1536 | bytes 6144
  30.3 38.2 %all-gather = bf16[1,3,2304]{1,0,2:T(2,128)(2,1)S(1)} all-gather(bf16[1,3,576]{1,0,2:T(2,128)(2,1)S(1)} %copy.47), channel_id=2, replica_groups=mesh['section'=2,'chan'=4,'dp'=4] {'chan'}, dimensions={2}, use_global_device_ids=true | all-gather | bytes 17280 | tf_op jit(solution)/shard_map/all_gather | solution.py:64
  70.3 68.9 %slice_reduce_fusion.2 = (f32[2304]{0:T(1024)S(1)}, f32[2304]{0:T(1024)S(1)}, f32[2304]{0:T(1024)S(1)}) fusion(f32[1,3,2304]{1,0,2:T(1,128)S(1)} %convert_element_type.178), kind=kLoop, calls=%fused_computation.125 | loop fusion | bytes 55296 | tf_op jit(solution)/shard_map/slice | solution.py:88
  142.5 8.9 %fusion.66 = f32[2048,768]{1,0:T(8,128)} fusion(bf16[2048,1024]{1,0:T(8,128)(2,1)} %constant.57.clone, bf16[1,1024,768]{1,2,0:T(8,128)(2,1)} %all-gather.14.cloned.1.call-done, f32[1024]{0:T(1024)S(1)} %multiply_exponential_fusion), kind=kOutput, calls=%fused_computation.111 | convolution fusion | flops 3223584768 | bytes 12062720 | tf_op jit(solution)/shard_map/dot_general | solution.py:24
  162.2 11.7 %fusion.64 = f32[2048,768]{1,0:T(8,128)} fusion(bf16[2048,1024]{1,0:T(8,128)(2,1)} %constant.57.clone, f32[1024,2304]{1,0:T(8,128)S(1)} %multiply_add_fusion), kind=kOutput, calls=%fused_computation.109 | convolution fusion | flops 3222798336 | bytes 16777216 | tf_op jit(solution)/shard_map/dot_general | solution.py:24
  180.8 7.5 fusion.58
  192.2 66.2 %all-gather.18.cloned.1.call-done = bf16[1,768,3072]{2,1,0:T(8,128)(2,1)} async-done(((bf16[1,192,3072]{2,1,0:T(8,128)(2,1)}), bf16[1,768,3072]{2,1,0:T(8,128)(2,1)}) %all-gather.18.cloned.1.call-update) | async-done | bytes 4718608 | tf_op jit(solution)/shard_map/all_gather | solution.py:61
  258.4 11.8 %multiply_convert_fusion = (bf16[1024,3072]{1,0:T(8,128)(2,1)}, f32[1024,3072]{1,0:T(8,128)}) fusion(bf16[1,768,3072]{2,1,0:T(8,128)(2,1)} %all-gather.18.cloned.1.call-done, bf16[1024,768]{0,1:T(8,128)(2,1)S(1)} %get-tuple-element.76, f32[768]{0:T(1024)S(1)} %mul.391, f32[1024]{0:T(1024)S(1)} %add_rsqrt_fusion, f32[1024]{0:T(1024)S(1)} %broadcast_multiply_fusion.5), kind=kOutput, calls=%fused_computation.7 | convolution fusion | flops 4851499008 | bytes 25177088 | tf_op jit(solution)/shard_map/dot_general | solution.py:24
  270.2 77.5 %all-gather.20.cloned.1.call-done = bf16[1,3072,768]{2,1,0:T(8,128)(2,1)} async-done(((bf16[1,768,768]{2,1,0:T(8,128)(2,1)}), bf16[1,3072,768]{2,1,0:T(8,128)(2,1)}) %all-gather.20.cloned.1.call-update) | async-done | bytes 4718608 | tf_op jit(solution)/shard_map/all_gather | solution.py:61
  347.7 12.2 %fusion.5 = bf16[1024,3072]{1,0:T(8,128)(2,1)S(1)} fusion(f32[1024,3072]{1,0:T(8,128)} %get-tuple-element.78, bf16[1,3072,768]{2,1,0:T(8,128)(2,1)} %all-gather.20.cloned.1.call-done, bf16[1,1,1024,768]{2,3,1,0:T(8,128)(2,1)S(1)} %copy-done.13, f32[1024]{0:T(1024)S(1)} %fusion.85), kind=kOutput, calls=%fused_computation.6 | convolution fusion | flops 4865654784 | bytes 25169920 | tf_op jit(solution)/shard_map/dot_general | solution.py:24
  383.9 7.6 fusion.70
  402.2 12.9 %bitcast_multiply_fusion.1 = (f32[1024,768]{1,0:T(8,128)}, f32[1024,768]{1,0:T(8,128)}) fusion(f32[1024,2304]{1,0:T(8,128)} %copy-done.6, f32[768,1024]{0,1:T(8,128)} %fusion.72, bf16[1024,1024]{1,0:T(8,128)(2,1)} %constant.70, f32[2048,768]{1,0:T(8,128)} %fusion.65, f32[2048,768]{1,0:T(8,128)} %fusion.66), kind=kOutput, calls=%fused_computation.87 | convolution fusion | flops 1617690624 | bytes 30408704 | tf_op jit(solution)/shard_map/dot_general | solution.py:24
  415.1 14.3 %multiply_reduce_fusion.2 = (bf16[2304]{0:T(1024)(128)(2,1)S(1)}, bf16[2304]{0:T(1024)(128)(2,1)S(1)}, bf16[2304]{0:T(1024)(128)(2,1)S(1)}, f32[1024,2304]{1,0:T(8,128)S(1)}) fusion(f32[1024,2304]{1,0:T(8,128)} %copy-done.5, f32[1024,768]{1,0:T(8,128)} %get-tuple-element.65, f32[1024,768]{1,0:T(8,128)} %get-tuple-element.64, f32[1024,768]{1,0:T(8,128)} %get-tuple-element.82), kind=kLoop, calls=%fused_computation.21 | loop fusion | flops 18867456 | bytes 28325376 | tf_op jit(solution)/shard_map/reduce_sum | solution.py:119
  440.3 9.2 %convolution_convert_fusion.1 = bf16[768,3072]{1,0:T(8,128)(2,1)} fusion(bf16[1024,3072]{1,0:T(8,128)(2,1)} %copy-done.32, bf16[1024,768]{0,1:T(8,128)(2,1)} %copy-done.7, f32[768]{0:T(1024)S(1)} %mul.391, f32[1024]{0:T(1024)S(1)} %add_rsqrt_fusion, f32[1024]{0:T(1024)S(1)} %broadcast_multiply_fusion.5), kind=kOutput, calls=%fused_computation.25 | convolution fusion | flops 4838129664 | bytes 12594176 | tf_op jit(solution)/shard_map/dot_general | solution.py:24
  449.6 9.1 %convolution_convert_fusion = bf16[3072,768]{1,0:T(8,128)(2,1)} fusion(bf16[1024,3072]{1,0:T(8,128)(2,1)} %get-tuple-element.77, bf16[1,1,1024,768]{2,3,1,0:T(8,128)(2,1)} %copy.68, f32[1024]{0:T(1024)S(1)} %fusion.85), kind=kOutput, calls=%fused_computation.24 | convolution fusion | flops 4836556800 | bytes 12587008 | tf_op jit(solution)/shard_map/dot_general | solution.py:24
  459.1 8.3 %fusion.48 = (bf16[768]{0:T(1024)(128)(2,1)S(1)}, f32[1024]{0:T(1024)S(1)}, f32[1024]{0:T(1024)S(1)}, f32[1024,768]{0,1:T(8,128)S(1)}) fusion(bf16[1,1,1024,768]{2,3,1,0:T(8,128)(2,1)} %copy-done.2, f32[1024]{0:T(1024)S(1)} %add_rsqrt_fusion.1, f32[1024]{0:T(1024)S(1)} %broadcast_multiply_fusion.6, f32[768]{0:T(1024)S(1)} %mul.390, ...), kind=kOutput, calls=%fused_computation.71 | convolution fusion | flops 3630953728 | bytes 12997120 | tf_op jit(solution)/shard_map/dot_general | solution.py:24
  470.0 10.0 %broadcast_select_fusion = (bf16[1024,768]{0,1:T(8,128)(2,1)}, bf16[1024,768]{0,1:T(8,128)(2,1)}) fusion(bf16[1024,768]{0,1:T(8,128)(2,1)S(1)} %copy-done.8, pred[]{:T(512)S(6)} %eq.3, bf16[1024,3072]{1,0:T(8,128)(2,1)} %get-tuple-element.77, bf16[1,3072,768]{2,1,0:T(8,128)(2,1)} %all-gather.20.cloned.1.call-done, f32[1024]{0:T(1024)S(1)} %fusion.85), kind=kOutput, calls=%fused_computation.119 | convolution fusion | flops 4835770368 | bytes 15732737 | tf_op jit(solution)/shard_map/dot_general | solution.py:24
  481.8 34.8 %reduce-scatter.9.cloned.1.call-done = bf16[192,2304]{1,0:T(8,128)(2,1)} async-done(((bf16[768,2304]{1,0:T(8,128)(2,1)}), bf16[192,2304]{1,0:T(8,128)(2,1)}) %reduce-scatter.9.cloned.1.call-update) | async-done | bytes 884752 | tf_op jit(solution)/shard_map/reduce_scatter | solution.py:136
  516.7 87.9 %reduce-scatter.15.cloned.1.call-done = bf16[192,3072]{1,0:T(8,128)(2,1)} async-done(((bf16[768,3072]{1,0:T(8,128)(2,1)}), bf16[192,3072]{1,0:T(8,128)(2,1)}) %reduce-scatter.15.cloned.1.call-update) | async-done | bytes 1179664 | tf_op jit(solution)/shard_map/reduce_scatter | solution.py:136
  604.5 88.0 %reduce-scatter.17.cloned.1.call-done = bf16[768,768]{1,0:T(8,128)(2,1)} async-done(((bf16[3072,768]{1,0:T(8,128)(2,1)}), bf16[768,768]{1,0:T(8,128)(2,1)}) %reduce-scatter.17.cloned.1.call-update) | async-done | bytes 1179664 | tf_op jit(solution)/shard_map/reduce_scatter | solution.py:136
  693.2 11.0 %all-reduce.10 = (bf16[768]{0:T(1024)(128)(2,1)S(1)}, bf16[768]{0:T(1024)(128)(2,1)S(1)}) all-reduce(bf16[768]{0:T(1024)(128)(2,1)S(1)} %get-tuple-element.45, bf16[768]{0:T(1024)(128)(2,1)S(1)} %get-tuple-element.43), channel_id=8, replica_groups=mesh['section'=2,'chan'=4,'dp'=4] {'chan'}, use_global_device_ids=true, to_apply=%region_9.10.clone | all-reduce | flops 1536 | bytes 6144
  704.4 13.5 %reduce-scatter.19.cloned.1.call-done = bf16[576,3]{1,0:T(8,128)(2,1)} async-done(((bf16[2304,3]{1,0:T(8,128)(2,1)}), bf16[576,3]{1,0:T(8,128)(2,1)}) %reduce-scatter.19.cloned.1.call-update) | async-done | bytes 3472
  718.9 15.6 %all-reduce.8 = (bf16[1,3,576]{2,1,0:T(4,128)(2,1)S(1)}, bf16[1,192]{1,0:T(2,128)(2,1)S(1)}, bf16[1,192]{1,0:T(2,128)(2,1)S(1)}) all-reduce(bf16[1,3,576]{2,1,0:T(4,128)(2,1)S(1)} %bitcast.153, bf16[1,192]{1,0:T(2,128)(2,1)S(1)} %broadcast_in_dim.68, ...), channel_id=1, replica_groups=mesh['section'=2,'chan'=4,'dp'=4] {'section','dp'}, use_global_device_ids=true, to_apply=%region_17.18 | all-reduce | flops 2112 | bytes 8448 | tf_op jit(solution)/shard_map/psum | solution.py:137
  755.9 43.5 %all-reduce.14.cloned.1.call-done = (bf16[1,192,2304]{2,1,0:T(8,128)(2,1)}, bf16[1,1024,192]{1,2,0:T(8,128)(2,1)}, bf16[1,192,768]{2,1,0:T(8,128)(2,1)}, bf16[1,...) async-done(((bf16[1,192,2304]{2,1,0:T(8,128)(2,1)}, bf16[1,1024,192]{1,2,0:T(8,128)(2,1)}, bf16[1,192,768]{2,1,0:T(8,128)(2,1)}, bf16[1,192,3072]{2,1,0:T(8,128)(2,1)}, ...) | async-done | bytes 3932176 | tf_op jit(solution)/shard_map/psum | solution.py:137
  (176 shorter events, 115.4 us)
Async XLA Ops:
  7.2 135.3 %all-gather.14.cloned.1.call-start = ((), (), s32[]{:S(2)}) async-start(), calls=%async_computation.12 | async-start | bytes 1966080 | tf_op jit(solution)/shard_map/all_gather | solution.py:64
  7.9 143.4 %all-gather.12.cloned.1.call-start = ((), (), s32[]{:S(2)}) async-start(), calls=%async_computation.11 | async-start | bytes 4423680 | tf_op jit(solution)/shard_map/all_gather | solution.py:61
  8.7 179.6 %all-gather.16.cloned.1.call-start = ((), (), s32[]{:S(2)}) async-start(), calls=%async_computation.13 | async-start | bytes 1474560 | tf_op jit(solution)/shard_map/all_gather | solution.py:61
  9.4 249.0 %all-gather.18.cloned.1.call-start = ((), (), s32[]{:S(2)}) async-start(), calls=%async_computation.14 | async-start | bytes 5898240 | tf_op jit(solution)/shard_map/all_gather | solution.py:61
  10.0 337.7 %all-gather.20.cloned.1.call-start = ((), (), s32[]{:S(2)}) async-start(), calls=%async_computation.15 | async-start | bytes 5898240 | tf_op jit(solution)/shard_map/all_gather | solution.py:61
  10.6 471.2 %reduce-scatter.13.cloned.1.call-start = ((), (), s32[]{:S(2)}) async-start(), calls=%async_computation.8 | async-start | bytes 1474560 | tf_op jit(solution)/shard_map/reduce_scatter | solution.py:136
  11.9 18.1 %copy-start.25 = (bf16[1,3,576]{2,1,0:T(4,128)(2,1)S(1)}, bf16[1,3,576]{2,1,0:T(4,128)(2,1)}, u32[]{:S(2)}) copy-start(bf16[1,3,576]{2,1,0:T(4,128)(2,1)} %param.17) | copy-start | bytes 10372
  13.7 174.6 %copy-start.2 = (bf16[1,1,1024,768]{2,3,1,0:T(8,128)(2,1)}, bf16[1,1,1024,768]{2,3,1,0:T(8,128)(2,1)S(1)}, u32[]{:S(2)}) copy-start(bf16[1,1,1024,768]{2,3,1,0:T(8,128)(2,1)S(1)} %copy.67) | copy-start | bytes 4718596
  68.5 70.8 %copy-start.29 = (s32[2,1]{0,1:T(1,128)S(1)}, s32[2,1]{0,1:T(1,128)}, u32[]{:S(2)}) copy-start(s32[2,1]{0,1:T(1,128)} %param.13) | copy-start | bytes 28
  68.5 72.0 %copy-start.22 = (bf16[2,1,1024,768]{3,2,1,0:T(8,128)(2,1)S(1)}, bf16[2,1,1024,768]{3,2,1,0:T(8,128)(2,1)}, u32[]{:S(2)}) copy-start(bf16[2,1,1024,768]{3,2,1,0:T(8,128)(2,1)} %param.14) | copy-start | bytes 9437188
  157.6 16.4 %slice-start = ((s8[6291456]{0:T(1024)(128)(4,1)}), s8[4194304]{0:T(1024)(128)(4,1)S(1)}, s32[]{:S(2)}) async-start(s8[6291456]{0:T(1024)(128)(4,1)} %bitcast.142), calls=%async_computation.18 | async-start | bytes 8388608
  162.2 18.5 %copy-start.6 = (f32[1024,2304]{1,0:T(8,128)}, f32[1024,2304]{1,0:T(8,128)S(1)}, u32[]{:S(2)}) copy-start(f32[1024,2304]{1,0:T(8,128)S(1)} %multiply_add_fusion) | copy-start | bytes 28311556
  191.7 168.3 %copy-start.7 = (bf16[1024,768]{0,1:T(8,128)(2,1)}, bf16[1024,768]{0,1:T(8,128)(2,1)S(1)}, u32[]{:S(2)}) copy-start(bf16[1024,768]{0,1:T(8,128)(2,1)S(1)} %get-tuple-element.76) | copy-start | bytes 4718596
  192.2 155.5 %copy-start.13 = (bf16[1,1,1024,768]{2,3,1,0:T(8,128)(2,1)S(1)}, bf16[1,1,1024,768]{2,3,1,0:T(8,128)(2,1)}, u32[]{:S(2)}) copy-start(bf16[1,1,1024,768]{2,3,1,0:T(8,128)(2,1)} %copy.68) | copy-start | bytes 4718596
  347.7 12.2 %copy-start.15 = (bf16[1,768,3072]{2,1,0:T(8,128)(2,1)S(1)}, bf16[1,768,3072]{2,1,0:T(8,128)(2,1)}, u32[]{:S(2)}) copy-start(bf16[1,768,3072]{2,1,0:T(8,128)(2,1)} %all-gather.18.cloned.1.call-done) | copy-start | bytes 14155780
  383.9 98.0 %reduce-scatter.11.cloned.1.call-start = ((), (), s32[]{:S(2)}) async-start(), calls=%async_computation.7 | async-start | bytes 1966080 | tf_op jit(solution)/shard_map/reduce_scatter | solution.py:136
  383.9 14.9 %slice-start.2 = ((s8[6291456]{0:T(1024)(128)(4,1)}), s8[4194304]{0:T(1024)(128)(4,1)S(1)}, s32[]{:S(2)}) async-start(s8[6291456]{0:T(1024)(128)(4,1)} %bitcast.145), calls=%async_computation.20 | async-start | bytes 8388608
  415.1 101.6 %reduce-scatter.9.cloned.1.call-start = ((), (), s32[]{:S(2)}) async-start(), calls=%async_computation.6 | async-start | bytes 4423680 | tf_op jit(solution)/shard_map/reduce_scatter | solution.py:136
  440.3 164.3 %reduce-scatter.15.cloned.1.call-start = ((), (), s32[]{:S(2)}) async-start(), calls=%async_computation.9 | async-start | bytes 5898240 | tf_op jit(solution)/shard_map/reduce_scatter | solution.py:136
  449.5 243.0 %reduce-scatter.17.cloned.1.call-start = ((), (), s32[]{:S(2)}) async-start(), calls=%async_computation.10 | async-start | bytes 5898240 | tf_op jit(solution)/shard_map/reduce_scatter | solution.py:136
  458.7 259.2 %reduce-scatter.19.cloned.1.call-start = ((), (), s32[]{:S(2)}) async-start(), calls=%async_computation.16 | async-start | bytes 737280
  469.9 266.3 %collective-permute-start.1 = (bf16[1024,768]{0,1:T(8,128)(2,1)}, bf16[1024,768]{0,1:T(8,128)(2,1)}, u32[]{:S(2)}, u32[]{:S(2)}) collective-permute-start(bf16[1024,768]{0,1:T(8,128)(2,1)} %select_convert_fusion), channel_id=1, source_target_pairs={{0,16},{16,0},{1,17},{17,1},{2,18},{18,2},{3,19},{19,3},{4,20},{20... | collective-permute-start | bytes 4718600 | tf_op jit(solution)/shard_map/ppermute | solution.py:131
  480.0 271.1 %collective-permute-start = (bf16[1024,768]{0,1:T(8,128)(2,1)}, bf16[1024,768]{0,1:T(8,128)(2,1)}, u32[]{:S(2)}, u32[]{:S(2)}) collective-permute-start(bf16[1024,768]{0,1:T(8,128)(2,1)} %get-tuple-element.79), channel_id=1, source_target_pairs={{0,16},{16,0},{1,17},{17,1},{2,18},{18,2},{3,19},{19,3},{4,20},{20... | collective-permute-start | bytes 4718600 | tf_op jit(solution)/shard_map/ppermute | solution.py:131
  481.7 317.6 %all-reduce.14.cloned.1.call-start = ((), (), s32[]{:S(2)}) async-start(), calls=%async_computation.17 | async-start | bytes 7864320 | tf_op jit(solution)/shard_map/psum | solution.py:137
  (27 other events, 137.3 us)
Sparse Core Ops, SparseCore 0:
  9.6 58.1 all-gather.13
  69.3 68.3 all-gather.11
  139.3 29.0 all-gather.15
  169.8 88.5 all-gather.17
  259.8 87.8 all-gather.19
  384.0 27.6 reduce-scatter.12
  415.2 33.7 reduce-scatter.10
  451.3 65.3 reduce-scatter.8
  519.0 85.5 reduce-scatter.14
  606.7 85.7 reduce-scatter.16
  695.4 22.5 reduce-scatter.18
  721.7 77.6 all-reduce.13
